TPU v7x, 256 devices: a whole 4x4x8 slice. The times are simulated.
256 devices in a mesh: pole: 4 (over z_lo), prow: 8 (over x, core), pcol: 8 (over y, z_hi).
Axes of the slice: x: 4, y: 4, z: 8 (z_hi: 2, z_lo: 4; z = z_hi * 4 + z_lo), core: 2. Of those that a mesh axis runs over, the one named last changes fastest.
Arguments:
- lower: float32 [4, 4096, 4096], P('pole', 'prow', 'pcol'), may hold values from -0.1875 to 0.1875
- upper: float32 [4, 4096, 4096], P('pole', 'prow', 'pcol'), may hold values from -0.1875 to 0.1875
- dinv: float32 [4, 4096, 4096], P('pole', 'prow', 'pcol'), may hold values from -6 to 6
- pole_weight: float32 [4], P('pole'), may hold values from 0.25 to 1
- block_pattern: int32 [16, 16], replicated, may hold values 0 or 1
Outputs:
- density: float32 [4096, 4096], P('prow', 'pcol')
All inputs are finite; a program needn't handle non-finite values.
Results may differ from a plain program's by a relative error of at most 0.0001.
Values sent between devices are 32-bit elements; how exact they have to be, the bound alone decides.
A program may use at most 64 MiB of HBM per device.

v0:
```python
import jax
import jax.numpy as jnp
from jax import lax
from jax.sharding import PartitionSpec as P

B = 256


def tier_of(supers):
    halves = supers // 2
    upper_tier = jnp.where(halves < 4, 1, 2)
    return jnp.where(supers % 2 == 0, 0, upper_tier)


def node_of(supers):
    halves = supers // 2
    upper_node = jnp.where(halves < 4, halves // 2, 0)
    return jnp.where(supers % 2 == 0, halves // 2, upper_node)


def above(elders, youngers):
    tier_old = tier_of(elders)[:, None]
    tier_new = tier_of(youngers)[None, :]
    node_old = node_of(elders)[:, None]
    node_new = node_of(youngers)[None, :]
    shift_by = jnp.maximum(tier_old - tier_new, 0)
    return (tier_old > tier_new) & (node_old == jnp.right_shift(node_new, shift_by))


def same_node(firsts, seconds):
    tier_same = tier_of(firsts)[:, None] == tier_of(seconds)[None, :]
    node_same = node_of(firsts)[:, None] == node_of(seconds)[None, :]
    return tier_same & node_same


def highest(left, right):
    return jnp.dot(left, right, precision=lax.Precision.HIGHEST, preferred_element_type=jnp.float32)


def blockmul(values, mask):
    mask_rows, mask_cols = mask.shape
    shaped = values.reshape(
        mask_rows, values.shape[0] // mask_rows, mask_cols, values.shape[1] // mask_cols
    )
    return (shaped * mask[:, None, :, None].astype(values.dtype)).reshape(values.shape)


def quarter(values, row_slot, col_slot):
    height, breadth = values.shape
    shaped = values.reshape(height // (2 * B), 2, B, breadth // (2 * B), 2, B)
    return shaped[:, row_slot, :, :, col_slot, :].reshape(height // 2, breadth // 2)


def rows_in_slot(values, slot_now):
    height, breadth = values.shape
    return values.reshape(height // (2 * B), 2, B, breadth)[:, slot_now].reshape(
        height // 2, breadth
    )


def columns_in_slot(values, slot_now):
    height, breadth = values.shape
    return values.reshape(height, breadth // (2 * B), 2, B)[:, :, slot_now].reshape(
        height, breadth // 2
    )


def assemble(part_even, part_mixed, part_cross, part_odd):
    half_rows, half_cols = part_even.shape
    shape_four = (half_rows // B, B, half_cols // B, B)
    top_half = jnp.stack([part_even.reshape(shape_four), part_mixed.reshape(shape_four)], axis=3)
    bottom_half = jnp.stack([part_cross.reshape(shape_four), part_odd.reshape(shape_four)], axis=3)
    return jnp.stack([top_half, bottom_half], axis=1).reshape(2 * half_rows, 2 * half_cols)


def local(lower, upper, dinv, pole_weight, block_pattern):
    height, breadth = (lower.shape[1], lower.shape[2])
    row_blocks = height // B
    col_blocks = breadth // B
    row_sup = lax.axis_index("prow") * row_blocks + jnp.arange(row_blocks)
    col_sup = lax.axis_index("pcol") * col_blocks + jnp.arange(col_blocks)
    pattern_here = lax.dynamic_slice(
        block_pattern, (row_sup[0], col_sup[0]), (row_blocks, col_blocks)
    )
    pattern_flip = lax.dynamic_slice(
        block_pattern, (col_sup[0], row_sup[0]), (col_blocks, row_blocks)
    ).T
    keep_lower = above(row_sup, col_sup) & (pattern_here > 0)
    keep_upper = above(col_sup, row_sup).T & (pattern_flip > 0)
    row_odd = row_sup[1::2]
    col_odd = col_sup[1::2]
    root_mask = same_node(row_odd, col_odd) & (tier_of(row_odd)[:, None] == 2)
    empty = jnp.zeros((height // 2, breadth // 2), jnp.float32)
    weight = pole_weight[0]
    lmat = blockmul(lower[0], keep_lower)
    umat = blockmul(upper[0], keep_upper)
    lower_panel = lax.all_gather(rows_in_slot(lmat, 1), "prow", axis=0, tiled=True)
    upper_panel = lax.all_gather(columns_in_slot(umat, 1), "pcol", axis=1, tiled=True)
    greens_odd = blockmul(quarter(dinv[0], 1, 1), root_mask)
    panel = empty
    rowpart = empty
    diagpart = empty
    for tier_now in (1, 0):
        slot_now = 0 if tier_now == 0 else 1
        row_tier = row_sup[slot_now::2]
        col_tier = col_sup[slot_now::2]
        left_factor = columns_in_slot(lower_panel, slot_now)
        right_factor = rows_in_slot(upper_panel, slot_now)

        def along_columns(piece):
            return highest(right_factor, piece)

        folded_rows = highest(lax.all_gather(greens_odd, "pcol", axis=1, tiled=True), left_factor)
        col_flags = tier_of(col_tier) == tier_now
        row_flags = tier_of(row_tier) == tier_now
        panel = -blockmul(folded_rows, above(row_odd, col_tier) & col_flags[None, :])
        folded_columns = along_columns(lax.all_gather(greens_odd, "prow", axis=0, tiled=True))
        rowpart = -blockmul(folded_columns, above(col_odd, row_tier).T & row_flags[:, None])
        correction = along_columns(lax.all_gather(panel, "prow", axis=0, tiled=True))
        share = same_node(row_tier, col_tier) & row_flags[:, None]
        diagpart = blockmul(quarter(dinv[0], slot_now, slot_now) - correction, share)
        if tier_now > 0:
            greens_odd = greens_odd + panel + rowpart + diagpart
    density = weight * assemble(diagpart, rowpart, panel, greens_odd)
    return lax.psum(density, "pole")


def solution(mesh):
    in_specs = (
        P("pole", "prow", "pcol"),
        P("pole", "prow", "pcol"),
        P("pole", "prow", "pcol"),
        P("pole"),
        P(),
    )
    out_specs = P("prow", "pcol")
    return jax.shard_map(local, mesh=mesh, in_specs=in_specs, out_specs=out_specs, check_vma=False)
```

profile of v0, /device:TPU:1, one launch (start us, length us, event | category | flops | bytes accessed | tf_op | source)
XLA Modules:
  0.0 553.8 jit_solution(16048855129079267908)
XLA Ops:
  6.6 0.6 fusion.72
  8.6 0.6 fusion.71
  10.5 0.1 broadcast_subtract_fusion
  10.6 0.1 copy.16
  12.0 0.8 fusion.67
  12.8 0.1 copy.19
  12.9 0.8 and_convert_fusion
  13.7 0.1 broadcast_bitcast_fusion
  13.8 1.9 slice_multiply_fusion
  15.7 0.0 all-gather.11.cloned.1.call-start
  21.1 0.7 reshape_squeeze.33
  21.8 0.5 fusion.70
  22.2 0.7 fusion.66
  23.0 0.0 all-gather.23.cloned.1.call-start
  23.0 0.1 copy.14
  23.1 0.1 slice.61
  23.3 0.7 reshape_squeeze.35
  24.0 1.5 slice_multiply_fusion.1
  25.5 0.0 all-gather.15.cloned.1.call-start
  25.6 29.1 %all-gather.25.cloned.1.call-done = f32[1,1,2048,512]{3,2,1,0:T(8,128)} async-done(((f32[1,1,256,512]{3,2,1,0:T(8,128)}), f32[1,1,2048,512]{3,2,1,0:T(8,128)}) %all-gather.25.cloned.1.call-update) | async-done | bytes 4194320 | tf_op jit(solution)/shard_map/all_gather | solution.py:97
  54.7 5.9 %reshape.388 = f32[2048,1,2,256]{3,2,0,1:T(2,128)} reshape(f32[1,1,2048,512]{3,2,1,0:T(8,128)} %all-gather.25.cloned.1.call-done) | data formatting | bytes 8388608 | tf_op jit(solution)/shard_map/reshape | solution.py:63
  60.6 7.6 %fusion.69 = (f32[2048,1,1,256]{3,2,0,1:T(1,128)}, f32[2048,1,1,256]{3,2,0,1:T(1,128)S(1)}) fusion(f32[2048,1,2,256]{3,2,0,1:T(2,128)} %reshape.388), kind=kLoop, calls=%fused_computation.77 | loop fusion | bytes 8388608 | tf_op jit(solution)/shard_map/slice | solution.py:63
  68.2 64.3 %all-gather.11.cloned.1.call-done = f32[256,2048]{1,0:T(8,128)} async-done(((f32[256,256]{1,0:T(8,128)}), f32[256,2048]{1,0:T(8,128)}) %all-gather.11.cloned.1.call-update) | async-done | bytes 2097168 | tf_op jit(solution)/shard_map/all_gather | solution.py:113
  132.5 4.2 fusion.39
  136.7 0.0 all-gather.13.cloned.1.call-start
  136.8 0.5 all-gather.13.cloned.1.call-update
  137.3 0.2 all-gather.17.cloned.1.call-start
  137.6 144.1 %all-gather.23.cloned.1.call-done = f32[512,1,1,2048]{3,2,0,1:T(1,128)} async-done(((f32[512,1,1,256]{3,2,0,1:T(1,128)}), f32[512,1,1,2048]{3,2,0,1:T(1,128)}) %all-gather.23.cloned.1.call-update) | async-done | bytes 4194320 | tf_op jit(solution)/shard_map/all_gather | solution.py:98
  281.7 6.5 %fusion.68 = (f32[1,1,256,2048]{3,0,2,1:T(1,128)S(1)}, f32[1,1,256,2048]{3,0,2,1:T(1,128)}) fusion(f32[1,2,256,2048]{3,0,2,1:T(1,128)} %bitcast.118), kind=kLoop, calls=%fused_computation.76 | loop fusion | bytes 8388608 | tf_op jit(solution)/shard_map/slice | solution.py:56
  288.1 19.3 %all-gather.15.cloned.1.call-done = f32[2048,256]{1,0:T(8,128)} async-done(((f32[256,256]{1,0:T(8,128)}), f32[2048,256]{1,0:T(8,128)}) %all-gather.15.cloned.1.call-update) | async-done | bytes 2097168 | tf_op jit(solution)/shard_map/all_gather | solution.py:119
  307.4 4.6 fusion.57
  312.0 25.2 %all-gather.13.cloned.1.call-done = f32[2048,256]{1,0:T(8,128)} async-done(((f32[256,256]{1,0:T(8,128)}), f32[2048,256]{1,0:T(8,128)}) %all-gather.13.cloned.1.call-update) | async-done | bytes 2097168 | tf_op jit(solution)/shard_map/all_gather | solution.py:117
  337.2 5.2 fusion.51
  342.5 0.0 all-gather.21.cloned.1.call-start
  342.5 0.7 all-gather.21.cloned.1.call-update
  345.8 72.5 %all-gather.17.cloned.1.call-done = f32[256,2048]{1,0:T(8,128)} async-done(((f32[256,256]{1,0:T(8,128)}), f32[256,2048]{1,0:T(8,128)}) %all-gather.17.cloned.1.call-update) | async-done | bytes 2097168 | tf_op jit(solution)/shard_map/all_gather | solution.py:113
  418.3 4.9 fusion.63
  423.2 0.3 all-reduce.2.cloned.1.call-start
  426.9 1.0 maximum_bitcast_fusion.1
  427.9 17.4 %all-gather.21.cloned.1.call-done = f32[2048,256]{1,0:T(8,128)} async-done(((f32[256,256]{1,0:T(8,128)}), f32[2048,256]{1,0:T(8,128)}) %all-gather.21.cloned.1.call-update) | async-done | bytes 2097168 | tf_op jit(solution)/shard_map/all_gather | solution.py:117
  445.3 3.9 fusion.33
  449.2 26.0 %all-gather.19.cloned.1.call-done = f32[2048,256]{1,0:T(8,128)} async-done(((f32[256,256]{1,0:T(8,128)}), f32[2048,256]{1,0:T(8,128)}) %all-gather.19.cloned.1.call-update) | async-done | bytes 2097168 | tf_op jit(solution)/shard_map/all_gather | solution.py:119
  475.2 3.9 fusion.24
  479.2 0.1 maximum_multiply_fusion
  479.3 0.8 copy.20
  480.1 1.0 copy.30
  481.2 63.8 %all-reduce.2.cloned.1.call-done = f32[512,512]{1,0:T(8,128)} async-done(((f32[512,512]{1,0:T(8,128)}), f32[512,512]{1,0:T(8,128)}) %all-reduce.2.cloned.1.call-update) | async-done | bytes 1048592 | tf_op jit(solution)/shard_map/psum | solution.py:125
  545.0 2.3 copy.97
  (27 shorter events, 0.3 us)
Async XLA Ops:
  6.5 14.5 %copy-start.3 = (f32[1,512,512]{2,1,0:T(8,128)S(1)}, f32[1,512,512]{2,1,0:T(8,128)}, u32[]{:S(2)}) copy-start(f32[1,512,512]{2,1,0:T(8,128)} %param.7) | copy-start | bytes 3145732
  6.5 48.1 %all-gather.25.cloned.1.call-start = ((), (), s32[]{:S(2)}) async-start(), calls=%async_computation.8 | async-start | bytes 4718592 | tf_op jit(solution)/shard_map/all_gather | solution.py:97
  15.7 116.8 %all-gather.11.cloned.1.call-start = ((), (), s32[]{:S(2)}) async-start(), calls=%async_computation | async-start | bytes 2359296 | tf_op jit(solution)/shard_map/all_gather | solution.py:113
  21.7 1.5 copy-start.4
  23.0 258.7 %all-gather.23.cloned.1.call-start = ((), (), s32[]{:S(2)}) async-start(), calls=%async_computation.7 | async-start | bytes 4718592 | tf_op jit(solution)/shard_map/all_gather | solution.py:98
  25.5 281.9 %all-gather.15.cloned.1.call-start = ((), (), s32[]{:S(2)}) async-start(), calls=%async_computation.2 | async-start | bytes 2359296 | tf_op jit(solution)/shard_map/all_gather | solution.py:119
  136.7 200.5 %all-gather.13.cloned.1.call-start = ((), (), s32[]{:S(2)}) async-start(), calls=%async_computation.1 | async-start | bytes 2359296 | tf_op jit(solution)/shard_map/all_gather | solution.py:117
  137.3 280.9 %all-gather.17.cloned.1.call-start = ((), (), s32[]{:S(2)}) async-start(), calls=%async_computation.3 | async-start | bytes 2359296 | tf_op jit(solution)/shard_map/all_gather | solution.py:113
  307.4 29.8 %copy-start = (f32[256,256]{1,0:T(8,128)S(1)}, f32[256,256]{1,0:T(8,128)}, u32[]{:S(2)}) copy-start(f32[256,256]{1,0:T(8,128)} %fusion.66) | copy-start | bytes 786436
  307.4 29.8 %copy-start.2 = (f32[256,256]{1,0:T(8,128)S(1)}, f32[256,256]{1,0:T(8,128)}, u32[]{:S(2)}) copy-start(f32[256,256]{1,0:T(8,128)} %fusion.39) | copy-start | bytes 786436
  342.5 102.9 %all-gather.21.cloned.1.call-start = ((), (), s32[]{:S(2)}) async-start(), calls=%async_computation.5 | async-start | bytes 2359296 | tf_op jit(solution)/shard_map/all_gather | solution.py:117
  343.2 132.0 %all-gather.19.cloned.1.call-start = ((), (), s32[]{:S(2)}) async-start(), calls=%async_computation.4 | async-start | bytes 2359296 | tf_op jit(solution)/shard_map/all_gather | solution.py:119
  418.3 8.6 %copy-start.1 = (f32[256,256]{1,0:T(8,128)S(1)}, f32[256,256]{1,0:T(8,128)}, u32[]{:S(2)}) copy-start(f32[256,256]{1,0:T(8,128)} %fusion.51) | copy-start | bytes 786436
  423.2 121.9 %all-reduce.2.cloned.1.call-start = ((), (), s32[]{:S(2)}) async-start(), calls=%async_computation.6 | async-start | bytes 2097152 | tf_op jit(solution)/shard_map/psum | solution.py:125
Sparse Core Ops, SparseCore 0:
  15.8 38.8 all-gather.24
  57.2 75.3 all-gather.10
  135.0 146.6 all-gather.22
  283.4 24.0 all-gather.14
  309.1 28.0 all-gather.12
  342.6 75.6 all-gather.16
  420.1 25.1 all-gather.20
  447.2 28.0 all-gather.18
  481.3 63.6 all-reduce.1
where the time goes:
time: 555 us; the launch traced here: 554 us
  waiting for transfers between devices  463 us (83%)
  between operations  28.7 us (5%)
  local copies, waits for them, and re-layouts  27.7 us (5%)
  matrix products  26.7 us (5%)
  other arithmetic  6.91 us (1%)
    all_gather x1, waiting for transfers between devices, local(): lax.all_gather(columns_in_slot(umat, 1), 'pcol', axis=1, tiled=True)  144 us
    all_gather x2, waiting for transfers between devices, local(): lax.all_gather(greens_odd, 'pcol', axis=1, tiled=True)  137 us
    psum x1, waiting for transfers between devices, local(): return lax.psum(density, 'pole')  63.8 us
    all_gather x2, waiting for transfers between devices, local(): lax.all_gather(panel, 'prow', axis=0, tiled=True)  45.3 us
    all_gather x2, waiting for transfers between devices, local(): lax.all_gather(greens_odd, 'prow', axis=0, tiled=True)  42.6 us
    all_gather x1, waiting for transfers between devices, local(): lax.all_gather(rows_in_slot(lmat, 1), 'prow', axis=0, tiled=True)  29.1 us
    dot_general x6, matrix products, highest(): jnp.dot(left, right, precision=lax.Precision.HIGHEST, preferred_element_t...  26.7 us
  transfers between devices with their start and end apart: 9, of which 9 were waited for; matrix products, arithmetic and copies ran while one was open for 8% of the time, Pallas kernels for 0%

commit v1 on v0

--- a/solution.py
+++ b/solution.py
@@ -122,7 +122,7 @@
         if tier_now > 0:
             greens_odd = greens_odd + panel + rowpart + diagpart
     density = weight * assemble(diagpart, rowpart, panel, greens_odd)
-    return lax.psum(density, "pole")
+    return jnp.sum(lax.all_gather(density, "pole"), axis=0)
 
 
 def solution(mesh):

time: 555 us -> 577 us (1.040)
  waiting for transfers between devices: 463 us -> 483 us
    all_gather x0 -> x1, waiting for transfers between devices: none -> 84 us  [local(): return jnp.sum(lax.all_gather(density, 'pole'), axis=0)]
    psum x1 -> x0, waiting for transfers between devices: 63.8 us -> none  [local(): return lax.psum(density, 'pole')]
  transfers between devices with their start and end apart: 9 -> 9, of which waited for: 9 -> 9; matrix products, arithmetic and copies ran while one was open for 8% -> 7% of each run, Pallas kernels for 0% -> 0%
where the time goes in v1:
time: 577 us; the launch traced here: 576 us
  waiting for transfers between devices  483 us (84%)
  between operations  28.7 us (5%)
  matrix products  26.7 us (5%)
  local copies, waits for them, and re-layouts  26.2 us (5%)
  other arithmetic  10.6 us (2%)
    all_gather x1, waiting for transfers between devices, local(): lax.all_gather(columns_in_slot(umat, 1), 'pcol', axis=1, tiled=True)  144 us
    all_gather x2, waiting for transfers between devices, local(): lax.all_gather(greens_odd, 'pcol', axis=1, tiled=True)  137 us
    all_gather x1, waiting for transfers between devices, local(): return jnp.sum(lax.all_gather(density, 'pole'), axis=0)  84 us
    all_gather x2, waiting for transfers between devices, local(): lax.all_gather(panel, 'prow', axis=0, tiled=True)  45.3 us
    all_gather x2, waiting for transfers between devices, local(): lax.all_gather(greens_odd, 'prow', axis=0, tiled=True)  42.6 us
    all_gather x1, waiting for transfers between devices, local(): lax.all_gather(rows_in_slot(lmat, 1), 'prow', axis=0, tiled=True)  29.1 us
    dot_general x6, matrix products, highest(): jnp.dot(left, right, precision=lax.Precision.HIGHEST, preferred_element_t...  26.7 us
  transfers between devices with their start and end apart: 9, of which 9 were waited for; matrix products, arithmetic and copies ran while one was open for 7% of the time, Pallas kernels for 0%

profile of v1, /device:TPU:1, one launch (start us, length us, event | category | flops | bytes accessed | tf_op | source)
XLA Modules:
  0.0 576.2 jit_solution(8540137907187857277)
XLA Ops:
  6.6 0.6 fusion.72
  8.6 0.6 fusion.71
  10.5 0.1 broadcast_subtract_fusion
  10.6 0.1 copy.25
  12.0 0.8 fusion.67
  12.8 0.1 copy.28
  12.9 0.8 and_convert_fusion
  13.7 0.1 broadcast_bitcast_fusion
  13.8 1.9 slice_multiply_fusion
  15.7 0.0 all-gather.12.cloned.1.call-start
  21.1 0.7 reshape_squeeze.33
  21.8 0.5 fusion.70
  22.2 0.7 fusion.66
  23.0 0.0 all-gather.26.cloned.1.call-start
  23.0 0.1 copy.23
  23.1 0.1 slice.61
  23.3 0.7 reshape_squeeze.35
  24.0 1.5 slice_multiply_fusion.1
  25.5 0.0 all-gather.16.cloned.1.call-start
  25.6 29.1 %all-gather.28.cloned.1.call-done = f32[1,1,2048,512]{3,2,1,0:T(8,128)} async-done(((f32[1,1,256,512]{3,2,1,0:T(8,128)}), f32[1,1,2048,512]{3,2,1,0:T(8,128)}) %all-gather.28.cloned.1.call-update) | async-done | bytes 4194320 | tf_op jit(solution)/shard_map/all_gather | solution.py:97
  54.7 5.9 %reshape.398 = f32[2048,1,2,256]{3,2,0,1:T(2,128)} reshape(f32[1,1,2048,512]{3,2,1,0:T(8,128)} %all-gather.28.cloned.1.call-done) | data formatting | bytes 8388608 | tf_op jit(solution)/shard_map/reshape | solution.py:63
  60.6 7.6 %fusion.69 = (f32[2048,1,1,256]{3,2,0,1:T(1,128)}, f32[2048,1,1,256]{3,2,0,1:T(1,128)S(1)}) fusion(f32[2048,1,2,256]{3,2,0,1:T(2,128)} %reshape.398), kind=kLoop, calls=%fused_computation.77 | loop fusion | bytes 8388608 | tf_op jit(solution)/shard_map/slice | solution.py:63
  68.2 64.3 %all-gather.12.cloned.1.call-done = f32[256,2048]{1,0:T(8,128)} async-done(((f32[256,256]{1,0:T(8,128)}), f32[256,2048]{1,0:T(8,128)}) %all-gather.12.cloned.1.call-update) | async-done | bytes 2097168 | tf_op jit(solution)/shard_map/all_gather | solution.py:113
  132.5 4.2 fusion.39
  136.7 0.0 all-gather.14.cloned.1.call-start
  136.8 0.5 all-gather.14.cloned.1.call-update
  137.3 0.2 all-gather.18.cloned.1.call-start
  137.6 144.1 %all-gather.26.cloned.1.call-done = f32[512,1,1,2048]{3,2,0,1:T(1,128)} async-done(((f32[512,1,1,256]{3,2,0,1:T(1,128)}), f32[512,1,1,2048]{3,2,0,1:T(1,128)}) %all-gather.26.cloned.1.call-update) | async-done | bytes 4194320 | tf_op jit(solution)/shard_map/all_gather | solution.py:98
  281.7 6.5 %fusion.68 = (f32[1,1,256,2048]{3,0,2,1:T(1,128)S(1)}, f32[1,1,256,2048]{3,0,2,1:T(1,128)}) fusion(f32[1,2,256,2048]{3,0,2,1:T(1,128)} %bitcast.116), kind=kLoop, calls=%fused_computation.76 | loop fusion | bytes 8388608 | tf_op jit(solution)/shard_map/slice | solution.py:56
  288.1 19.3 %all-gather.16.cloned.1.call-done = f32[2048,256]{1,0:T(8,128)} async-done(((f32[256,256]{1,0:T(8,128)}), f32[2048,256]{1,0:T(8,128)}) %all-gather.16.cloned.1.call-update) | async-done | bytes 2097168 | tf_op jit(solution)/shard_map/all_gather | solution.py:119
  307.4 4.6 fusion.57
  312.0 25.2 %all-gather.14.cloned.1.call-done = f32[2048,256]{1,0:T(8,128)} async-done(((f32[256,256]{1,0:T(8,128)}), f32[2048,256]{1,0:T(8,128)}) %all-gather.14.cloned.1.call-update) | async-done | bytes 2097168 | tf_op jit(solution)/shard_map/all_gather | solution.py:117
  337.2 5.2 fusion.51
  342.5 0.0 all-gather.22.cloned.1.call-start
  342.5 0.7 all-gather.22.cloned.1.call-update
  345.8 72.5 %all-gather.18.cloned.1.call-done = f32[256,2048]{1,0:T(8,128)} async-done(((f32[256,256]{1,0:T(8,128)}), f32[256,2048]{1,0:T(8,128)}) %all-gather.18.cloned.1.call-update) | async-done | bytes 2097168 | tf_op jit(solution)/shard_map/all_gather | solution.py:113
  418.3 4.9 fusion.63
  423.2 0.3 all-gather.24.cloned.1.call-start
  426.9 1.0 maximum_bitcast_fusion.1
  427.9 17.4 %all-gather.22.cloned.1.call-done = f32[2048,256]{1,0:T(8,128)} async-done(((f32[256,256]{1,0:T(8,128)}), f32[2048,256]{1,0:T(8,128)}) %all-gather.22.cloned.1.call-update) | async-done | bytes 2097168 | tf_op jit(solution)/shard_map/all_gather | solution.py:117
  445.3 3.9 fusion.33
  449.2 26.0 %all-gather.20.cloned.1.call-done = f32[2048,256]{1,0:T(8,128)} async-done(((f32[256,256]{1,0:T(8,128)}), f32[2048,256]{1,0:T(8,128)}) %all-gather.20.cloned.1.call-update) | async-done | bytes 2097168 | tf_op jit(solution)/shard_map/all_gather | solution.py:119
  475.2 3.9 fusion.24
  479.2 0.1 maximum_multiply_fusion
  479.3 0.8 copy.29
  480.1 1.8 mul.195
  482.0 84.0 %all-gather.24.cloned.1.call-done = f32[4,512,512]{2,1,0:T(8,128)} async-done(((f32[1,512,512]{2,1,0:T(8,128)}), f32[4,512,512]{2,1,0:T(8,128)}) %all-gather.24.cloned.1.call-update) | async-done | bytes 4194320 | tf_op jit(solution)/shard_map/all_gather | solution.py:125
  566.0 3.7 reduce_sum.9
  (27 shorter events, 0.3 us)
Async XLA Ops:
  6.5 14.5 %copy-start.3 = (f32[1,512,512]{2,1,0:T(8,128)S(1)}, f32[1,512,512]{2,1,0:T(8,128)}, u32[]{:S(2)}) copy-start(f32[1,512,512]{2,1,0:T(8,128)} %param.7) | copy-start | bytes 3145732
  6.5 48.1 %all-gather.28.cloned.1.call-start = ((), (), s32[]{:S(2)}) async-start(), calls=%async_computation.8 | async-start | bytes 4718592 | tf_op jit(solution)/shard_map/all_gather | solution.py:97
  15.7 116.8 %all-gather.12.cloned.1.call-start = ((), (), s32[]{:S(2)}) async-start(), calls=%async_computation | async-start | bytes 2359296 | tf_op jit(solution)/shard_map/all_gather | solution.py:113
  21.7 1.5 copy-start.4
  23.0 258.7 %all-gather.26.cloned.1.call-start = ((), (), s32[]{:S(2)}) async-start(), calls=%async_computation.7 | async-start | bytes 4718592 | tf_op jit(solution)/shard_map/all_gather | solution.py:98
  25.5 281.9 %all-gather.16.cloned.1.call-start = ((), (), s32[]{:S(2)}) async-start(), calls=%async_computation.2 | async-start | bytes 2359296 | tf_op jit(solution)/shard_map/all_gather | solution.py:119
  136.7 200.5 %all-gather.14.cloned.1.call-start = ((), (), s32[]{:S(2)}) async-start(), calls=%async_computation.1 | async-start | bytes 2359296 | tf_op jit(solution)/shard_map/all_gather | solution.py:117
  137.3 280.9 %all-gather.18.cloned.1.call-start = ((), (), s32[]{:S(2)}) async-start(), calls=%async_computation.3 | async-start | bytes 2359296 | tf_op jit(solution)/shard_map/all_gather | solution.py:113
  307.4 29.8 %copy-start = (f32[256,256]{1,0:T(8,128)S(1)}, f32[256,256]{1,0:T(8,128)}, u32[]{:S(2)}) copy-start(f32[256,256]{1,0:T(8,128)} %fusion.66) | copy-start | bytes 786436
  307.4 29.8 %copy-start.2 = (f32[256,256]{1,0:T(8,128)S(1)}, f32[256,256]{1,0:T(8,128)}, u32[]{:S(2)}) copy-start(f32[256,256]{1,0:T(8,128)} %fusion.39) | copy-start | bytes 786436
  342.5 102.9 %all-gather.22.cloned.1.call-start = ((), (), s32[]{:S(2)}) async-start(), calls=%async_computation.5 | async-start | bytes 2359296 | tf_op jit(solution)/shard_map/all_gather | solution.py:117
  343.2 132.0 %all-gather.20.cloned.1.call-start = ((), (), s32[]{:S(2)}) async-start(), calls=%async_computation.4 | async-start | bytes 2359296 | tf_op jit(solution)/shard_map/all_gather | solution.py:119
  418.3 8.6 %copy-start.1 = (f32[256,256]{1,0:T(8,128)S(1)}, f32[256,256]{1,0:T(8,128)}, u32[]{:S(2)}) copy-start(f32[256,256]{1,0:T(8,128)} %fusion.51) | copy-start | bytes 786436
  423.2 142.8 %all-gather.24.cloned.1.call-start = ((), (), s32[]{:S(2)}) async-start(), calls=%async_computation.6 | async-start | bytes 5242880 | tf_op jit(solution)/shard_map/all_gather | solution.py:125
Sparse Core Ops, SparseCore 0:
  15.8 38.8 all-gather.27
  57.2 75.3 all-gather.11
  135.0 146.6 all-gather.25
  283.4 24.0 all-gather.15
  309.1 28.0 all-gather.13
  342.6 75.6 all-gather.17
  420.1 25.1 all-gather.21
  447.2 28.0 all-gather.19
  482.1 83.8 all-gather.23
